TPU v7x, 256 devices: a whole 4x4x8 slice. The times are simulated.
256 devices in a mesh: dp: 64 (over y, z, core), grp: 4 (over x).
Axes of the slice: x: 4, y: 4, z: 8, core: 2. Of those that a mesh axis runs over, the one named last changes fastest.
Arguments:
- embeddings: bfloat16 [196608, 768], P(('dp', 'grp'))
- cluster_ids: int32 [196608], P(('dp', 'grp')), may hold values from 0 to 511, as said below
Outputs:
- max_similarity: float32 [196608], P(('dp', 'grp'))
Inputs may be any that keep to these rules, and one draw needn't show every extreme that they name: `cluster_ids`: within the rows of one device, at most 24 rows belong to the clusters of any one group (cluster c belongs to group c // 8); in every draw some group receives exactly 24 rows from every device.
All inputs are finite; a program needn't handle non-finite values.
Results may differ from a plain program's by a relative error of at most 0.0003.
Values may be sent and summed in bfloat16 or wider, within the bound.
A program may use at most 64 MiB of HBM per device.

v0:
```python
import math

import jax
import jax.numpy as jnp
from jax import lax
from jax.sharding import PartitionSpec as P

CL_GRP = 8


def from_behind(x, axis, by):
    peers = lax.axis_size(axis)
    return lax.ppermute(x, axis, [(i, (i + by) % peers) for i in range(peers)])


def unit_scale(block):
    values = block.astype(jnp.float32)
    return lax.rsqrt(jnp.mean(values * values, axis=1) + 1e-06) / math.sqrt(block.shape[1])


def masked_cosines(own_rows, own_ids, own_scale, other_rows, other_ids, other_scale, exclude_self):
    products = lax.dot_general(
        own_rows, other_rows, (((1,), (1,)), ((), ())), preferred_element_type=jnp.float32
    )
    cosines = products * own_scale[:, None] * other_scale[None, :]
    same = (own_ids[:, None] == other_ids[None, :]) & (own_ids[:, None] >= 0)
    if exclude_self:
        extent = own_ids.shape[0]
        first_idx = lax.broadcasted_iota(jnp.int32, (extent, extent), 0)
        second_idx = lax.broadcasted_iota(jnp.int32, (extent, extent), 1)
        same = same & (first_idx != second_idx)
    return jnp.where(same, cosines, -1.0)


def on_device(embeddings, cluster_ids):
    row_count = embeddings.shape[0]
    dp_size = lax.axis_size("dp")
    grp_size = lax.axis_size("grp")
    capacity = max(2, 2 * row_count // dp_size)
    owners = cluster_ids // CL_GRP
    one_hot = (owners[:, None] == jnp.arange(dp_size, dtype=jnp.int32)[None, :]).astype(
        jnp.bfloat16
    )
    earlier = (
        lax.broadcasted_iota(jnp.int32, (row_count, row_count), 0)
        > lax.broadcasted_iota(jnp.int32, (row_count, row_count), 1)
    ).astype(jnp.bfloat16)
    before = jnp.dot(earlier, one_hot, preferred_element_type=jnp.float32)
    ranks = jnp.sum(before * one_hot.astype(jnp.float32), axis=1).astype(jnp.int32)
    slots = owners * capacity + ranks
    buffer_rows = (
        jnp.zeros((dp_size * capacity, embeddings.shape[1]), jnp.bfloat16).at[slots].set(embeddings)
    )
    buffer_ids = jnp.full((dp_size * capacity,), -1, jnp.int32).at[slots].set(cluster_ids)
    held_rows, held_ids = (
        lax.all_to_all(buffer_rows, "dp", split_axis=0, concat_axis=0, tiled=True),
        lax.all_to_all(buffer_ids, "dp", split_axis=0, concat_axis=0, tiled=True),
    )
    held_scale = unit_scale(held_rows)
    best_sim = jnp.max(
        masked_cosines(held_rows, held_ids, held_scale, held_rows, held_ids, held_scale, True),
        axis=1,
    )
    visitor = (held_rows, held_ids)
    for distance in range(1, grp_size):
        visitor = from_behind((visitor[0], visitor[1]), "grp", 1)
        tile_now = masked_cosines(
            held_rows, held_ids, held_scale, visitor[0], visitor[1], unit_scale(visitor[0]), False
        )
        best_sim = jnp.maximum(best_sim, jnp.max(tile_now, axis=1))
    answers = lax.all_to_all(best_sim, "dp", split_axis=0, concat_axis=0, tiled=True)
    return answers[slots]


def solution(mesh):
    placed = (P(("dp", "grp"), None), P(("dp", "grp")))
    return jax.shard_map(
        on_device, mesh=mesh, in_specs=placed, out_specs=P(("dp", "grp")), check_vma=False
    )
```

profile of v0, /device:TPU:1, one launch (start us, length us, event | category | flops | bytes accessed | tf_op | source)
XLA Modules:
  0.0 283.1 jit_solution(10051292298362863069)
XLA Ops:
  0.0 0.7 add_select_fusion
  0.7 0.4 fusion.9
  1.1 0.7 compare_select_fusion
  1.8 7.9 %scatter_custom_fusion.1 = bf16[1536,768]{1,0:T(8,128)(2,1)} fusion(s32[768]{0:T(1024)S(1)} %compare_select_fusion, bf16[768,768]{1,0:T(8,128)(2,1)} %param.2, bf16[]{:T(256)} %constant.39.clone.1), kind=kCustom, calls=%fused_computation.23 | custom fusion | bytes 2359808 | tf_op jit(solution)/shard_map/scatter | solution.py:52
  9.7 70.1 %all_to_all.30 = bf16[64,24,768]{2,1,0:T(8,128)(2,1)S(1)} all-to-all(bf16[64,24,768]{2,1,0:T(8,128)(2,1)} %bitcast.21), channel_id=1, replica_groups=mesh['dp'=64,'grp'=4] {'dp'}, dimensions={0} | all-to-all | bytes 4718592 | tf_op jit(solution)/shard_map/all_to_all | solution.py:56
  79.8 1.2 collective-permute-start.1
  81.0 52.5 %collective-permute-done.1 = bf16[1536,768]{1,0:T(8,128)(2,1)} collective-permute-done((bf16[1536,768]{1,0:T(8,128)(2,1)S(1)}, bf16[1536,768]{1,0:T(8,128)(2,1)}, u32[]{:S(2)}, u32[]{:S(2)}) %collective-permute-start.1) | collective-permute-done | bytes 2359328 | tf_op jit(solution)/shard_map/ppermute | solution.py:13
  133.5 3.5 %scatter_custom_fusion = s32[1536]{0:T(1024)S(1)} fusion(s32[768]{0:T(1024)S(1)} %compare_select_fusion, s32[768]{0:T(1024)} %param.3, s32[]{:T(128)} %constant.31.clone.1), kind=kCustom, calls=%fused_computation.44 | custom fusion | bytes 6656 | tf_op jit(solution)/shard_map/scatter | solution.py:54
  137.2 16.1 %all_to_all.31 = s32[64,24,1]{1,2,0:T(1,128)S(1)} all-to-all(s32[64,24,1]{1,2,0:T(1,128)S(1)} %bitcast.22), channel_id=1, replica_groups=mesh['dp'=64,'grp'=4] {'dp'}, dimensions={0} | all-to-all | bytes 12288 | tf_op jit(solution)/shard_map/all_to_all | solution.py:57
  153.3 0.5 broadcast.149
  153.8 0.7 reduce.7
  154.5 0.1 eq.29
  154.6 1.3 collective-permute-start
  155.9 30.9 %collective-permute-done = s32[1536]{0:T(1024)S(1)} collective-permute-done((s32[1536]{0:T(1024)S(1)}, s32[1536]{0:T(1024)S(1)}, u32[]{:S(2)}, u32[]{:S(2)}) %collective-permute-start) | collective-permute-done | bytes 6176 | tf_op jit(solution)/shard_map/ppermute | solution.py:13
  186.8 3.7 %collective-permute-done.2 = s32[1536]{0:T(1024)S(1)} collective-permute-done((s32[1536]{0:T(1024)S(1)}, s32[1536]{0:T(1024)S(1)}, u32[]{:S(2)}, u32[]{:S(2)}) %collective-permute-start.2) | collective-permute-done | bytes 6176 | tf_op jit(solution)/shard_map/ppermute | solution.py:13
  190.5 0.5 multiply_reduce_fusion.3
  191.0 0.1 div.44
  191.1 6.2 %select_reduce_fusion.3 = f32[1536]{0:T(1024)S(1)} fusion(bf16[1536,768]{1,0:T(8,128)(2,1)S(1)} %bitcast.17, f32[1536]{0:T(1024)S(1)} %div.44, s32[1536]{0:T(1024)S(1)} %eq.29, pred[1536]{0:T(1024)(128)(4,1)S(1)} %broadcast_compare_fusion), kind=kOutput, calls=%fused_computation.14 | convolution fusion | flops 3642751488 | bytes 2379264 | tf_op jit(solution)/shard_map/dot_general | solution.py:22
  197.3 2.2 multiply_reduce_fusion.2
  199.6 6.2 %select_reduce_fusion.2 = f32[1536]{0:T(1024)S(1)} fusion(s32[1536]{0:T(1024)S(1)} %eq.29, s32[1536]{0:T(1024)S(1)} %collective-permute-done, pred[1536]{0:T(1024)(128)(4,1)S(1)} %broadcast_compare_fusion, f32[1536]{0:T(1024)S(1)} %rsqrt_multiply_fusion.3, f32[1536]{0:T(1024)S(1)} %div.44, bf16[1536,768]{1,0:T(8,128)(2,1)S(1)} %bitcast.18, ...), kind=kOutput, calls=%fused_computation.13 | convolution fusion | flops 3638032896 | bytes 4750848 | tf_op jit(solution)/shard_map/dot_general | solution.py:22
  205.8 2.2 multiply_reduce_fusion.1
  208.0 6.2 %select_reduce_fusion.1 = f32[1536]{0:T(1024)S(1)} fusion(s32[1536]{0:T(1024)S(1)} %eq.29, s32[1536]{0:T(1024)S(1)} %collective-permute-done.2, pred[1536]{0:T(1024)(128)(4,1)S(1)} %broadcast_compare_fusion, f32[1536]{0:T(1024)S(1)} %rsqrt_multiply_fusion.2, f32[1536]{0:T(1024)S(1)} %div.44, bf16[1536,768]{1,0:T(8,128)(2,1)S(1)} %bitcast.19, ...), kind=kOutput, calls=%fused_computation.12 | convolution fusion | flops 3638032896 | bytes 4750848 | tf_op jit(solution)/shard_map/dot_general | solution.py:22
  214.2 36.4 %collective-permute-done.5 = bf16[1536,768]{1,0:T(8,128)(2,1)S(1)} collective-permute-done((bf16[1536,768]{1,0:T(8,128)(2,1)}, bf16[1536,768]{1,0:T(8,128)(2,1)S(1)}, u32[]{:S(2)}, u32[]{:S(2)}) %collective-permute-start.5) | collective-permute-done | bytes 2359328 | tf_op jit(solution)/shard_map/ppermute | solution.py:13
  250.5 0.5 multiply_reduce_fusion
  251.1 4.9 %select_reduce_fusion = f32[1536]{0:T(1024)S(1)} fusion(s32[1536]{0:T(1024)S(1)} %eq.29, s32[1536]{0:T(1024)S(1)} %collective-permute-done.4, pred[1536]{0:T(1024)(128)(4,1)S(1)} %broadcast_compare_fusion, f32[1536]{0:T(1024)S(1)} %rsqrt_multiply_fusion.1, f32[1536]{0:T(1024)S(1)} %div.44, bf16[1536,768]{1,0:T(8,128)(2,1)S(1)} %bitcast.20, ...), kind=kOutput, calls=%fused_computation.11 | convolution fusion | flops 3638032896 | bytes 4750848 | tf_op jit(solution)/shard_map/dot_general | solution.py:22
  256.0 0.7 max.38
  256.7 9.6 %all-to-all-start.2 = ((f32[64,24,1]{1,2,0:T(1,128)}), f32[64,24,1]{1,2,0:T(1,128)S(1)}, u32[]{:S(2)}, u32[]{:S(2)}) async-start(f32[64,24,1]{1,2,0:T(1,128)} %bitcast.3), calls=%async_computation.2 | async-start | bytes 65536 | tf_op jit(solution)/shard_map/all_to_all | solution.py:71
  266.3 9.3 %all-to-all-done.2 = f32[64,24,1]{1,2,0:T(1,128)S(1)} async-done(((f32[64,24,1]{1,2,0:T(1,128)}), f32[64,24,1]{1,2,0:T(1,128)S(1)}, u32[]{:S(2)}, u32[]{:S(2)}) %all-to-all-start.2) | async-done | bytes 6176 | tf_op jit(solution)/shard_map/all_to_all | solution.py:71
  275.6 0.5 broadcast.150
  276.1 0.7 reduce.8
  276.8 0.1 all_to_all.26
  276.9 6.1 %gather_fusion = f32[768]{0:T(1024)} fusion(f32[1536]{0:T(1024)S(1)} %all_to_all.26, s32[1024]{0:T(1024)S(1)} %pad_clamp_fusion), kind=kCustom, calls=%fused_computation | custom fusion | bytes 9216 | tf_op jit(solution)/shard_map/gather | solution.py:72
  (14 shorter events, 0.2 us)
Async XLA Ops:
  79.8 53.7 %collective-permute-start.1 = (bf16[1536,768]{1,0:T(8,128)(2,1)S(1)}, bf16[1536,768]{1,0:T(8,128)(2,1)}, u32[]{:S(2)}, u32[]{:S(2)}) collective-permute-start(bf16[1536,768]{1,0:T(8,128)(2,1)S(1)} %bitcast.16), channel_id=1, source_target_pairs={{0,1},{1,2},{2,3},{3,0},{4,5},{5,6},{6,7},{7,4},{8,9},{9,10},{10,1... | collective-permute-start | bytes 7077896 | tf_op jit(solution)/shard_map/ppermute | solution.py:13
  133.5 65.9 %collective-permute-start.3 = (bf16[1536,768]{1,0:T(8,128)(2,1)}, bf16[1536,768]{1,0:T(8,128)(2,1)}, u32[]{:S(2)}, u32[]{:S(2)}) collective-permute-start(bf16[1536,768]{1,0:T(8,128)(2,1)} %collective-permute-done.1), channel_id=1, source_target_pairs={{0,1},{1,2},{2,3},{3,0},{4,5},{5,6},{6,7},{7,4},{8,9},{9,10},{10,1... | collective-permute-start | bytes 7077896 | tf_op jit(solution)/shard_map/ppermute | solution.py:13
  154.6 32.2 %collective-permute-start = (s32[1536]{0:T(1024)S(1)}, s32[1536]{0:T(1024)S(1)}, u32[]{:S(2)}, u32[]{:S(2)}) collective-permute-start(s32[1536]{0:T(1024)S(1)} %eq.29), channel_id=1, source_target_pairs={{0,1},{1,2},{2,3},{3,0},{4,5},{5,6},{6,7},{7,4},{8,9},{9,10},{10,1... | collective-permute-start | bytes 18440 | tf_op jit(solution)/shard_map/ppermute | solution.py:13
  186.8 3.7 %collective-permute-start.2 = (s32[1536]{0:T(1024)S(1)}, s32[1536]{0:T(1024)S(1)}, u32[]{:S(2)}, u32[]{:S(2)}) collective-permute-start(s32[1536]{0:T(1024)S(1)} %collective-permute-done), channel_id=1, source_target_pairs={{0,1},{1,2},{2,3},{3,0},{4,5},{5,6},{6,7},{7,4},{8,9},{9,10},{10,1... | collective-permute-start | bytes 18440 | tf_op jit(solution)/shard_map/ppermute | solution.py:13
  190.5 60.6 %collective-permute-start.4 = (s32[1536]{0:T(1024)S(1)}, s32[1536]{0:T(1024)S(1)}, u32[]{:S(2)}, u32[]{:S(2)}) collective-permute-start(s32[1536]{0:T(1024)S(1)} %collective-permute-done.2), channel_id=1, source_target_pairs={{0,1},{1,2},{2,3},{3,0},{4,5},{5,6},{6,7},{7,4},{8,9},{9,10},{10,1... | collective-permute-start | bytes 18440 | tf_op jit(solution)/shard_map/ppermute | solution.py:13
  199.5 51.0 %collective-permute-start.5 = (bf16[1536,768]{1,0:T(8,128)(2,1)}, bf16[1536,768]{1,0:T(8,128)(2,1)S(1)}, u32[]{:S(2)}, u32[]{:S(2)}) collective-permute-start(bf16[1536,768]{1,0:T(8,128)(2,1)} %collective-permute-done.3), channel_id=1, source_target_pairs={{0,1},{1,2},{2,3},{3,0},{4,5},{5,6},{6,7},{7,4},{8,9},{9,10},{10,1... | collective-permute-start | bytes 7077896 | tf_op jit(solution)/shard_map/ppermute | solution.py:13
  256.7 18.9 %all-to-all-start.2 = ((f32[64,24,1]{1,2,0:T(1,128)}), f32[64,24,1]{1,2,0:T(1,128)S(1)}, u32[]{:S(2)}, u32[]{:S(2)}) async-start(f32[64,24,1]{1,2,0:T(1,128)} %bitcast.3), calls=%async_computation.2 | async-start | bytes 65536 | tf_op jit(solution)/shard_map/all_to_all | solution.py:71
where the time goes:
time: 284 us; the launch traced here: 283 us
  waiting for transfers between devices  133 us (47%)
  blocking collectives  86.2 us (30%)
  matrix products  23.8 us (8%)
  local copies, waits for them, and re-layouts  19.7 us (7%)
  starting transfers between devices  12.2 us (4%)
  other arithmetic  8.34 us (3%)
    ppermute x6, waiting for transfers between devices, from_behind(): return lax.ppermute(x, axis, [(i, (i + by) % peers) for i in range(peers)])  123 us
    all_to_all x1, blocking collectives, on_device(): lax.all_to_all(buffer_rows, 'dp', split_axis=0, concat_axis=0, tiled=True)  70.1 us
    dot_general x4, matrix products, masked_cosines(): lax.dot_general(own_rows, other_rows, (((1,), (1,)), ((), ())), preferred...  23.4 us
    all_to_all x1, blocking collectives, on_device(): lax.all_to_all(buffer_ids, 'dp', split_axis=0, concat_axis=0, tiled=True)  16.1 us
    all_to_all x1, starting transfers between devices, on_device(): lax.all_to_all(best_sim, 'dp', split_axis=0, concat_axis=0, tiled=True)  9.61 us
    all_to_all x1, waiting for transfers between devices, on_device(): lax.all_to_all(best_sim, 'dp', split_axis=0, concat_axis=0, tiled=True)  9.27 us
    scatter x1, local copies, waits for them, and re-layouts, on_device(): jnp.zeros((dp_size * capacity, embeddings.shape[1]), jnp.bfloat16).at[slots]  7.93 us
    gather x1, local copies, waits for them, and re-layouts, on_device(): return answers[slots]  6.15 us
  transfers between devices with their start and end apart: 7, of which 5 were waited for; matrix products, arithmetic and copies ran while one was open for 10% of the time, Pallas kernels for 0%

commit v1 on v0

v1 whole, which is shorter than its diff:
```python
import math

import jax
import jax.numpy as jnp
from jax import lax
from jax.experimental import pallas as pl
from jax.experimental.pallas import tpu as pltpu
from jax.sharding import PartitionSpec as P

D = 768
RD = 768
G = 64
CAP = 24
NCH = 8
SRC = 16
B = SRC * CAP
MESH = pl.DeviceIdType.MESH
F32, BF16 = jnp.float32, jnp.bfloat16


def place(x, y, z, c):
    return ((y * 8 + z) * 2 + c, x)


def local_wait(ref, sem):
    pltpu.make_async_copy(ref, ref, sem).wait()


def pair_max(v, scale_col, id_col, scale_row, id_row, itself=None):
    row, cols = None, []
    for t in range(v.shape[1] // 128):
        at = slice(128 * t, 128 * (t + 1))
        same = id_col == id_row[:, at]
        if itself is not None:
            same = same & ~itself[:, at]
        m = jnp.where(same, v[:, at] * scale_col * scale_row[:, at], -1.0)
        row = m if row is None else jnp.maximum(row, m)
        cols.append(jnp.max(m, axis=0, keepdims=True))
    return row, jnp.concatenate(cols, axis=1)


def nt(a, b):
    return lax.dot_general(a, b, (((1,), (1,)), ((), ())), preferred_element_type=F32)


def kernel(
    ids_ref, emb_ref, out_ref,
    send, idsend, onehot, lanes, recv, idrecv, joint, meta, colmax, theirs, answer, back, scol, icol, rowmax,
    s_rows, s_ids, r_rows, r_ids, s_joint, s_meta, r_joint, r_meta, s_part, r_part, s_ans, r_ans,
):
    dp, x = lax.axis_index("dp"), lax.axis_index("grp")
    y, z, c = dp // 16, (dp // 2) % 8, dp % 2
    zh, par = z // 2, z % 2
    owner = (x + y + z) % 2 == 0
    other = place(x, y, z, 1 - c)

    barrier = pltpu.get_barrier_semaphore()

    @pl.when(owner)
    def _():
        @pl.loop(1, 128)
        def _(t):
            d = place((x + t // 32) % 4, (y + t // 8) % 4, (z + t) % 8, c)
            pl.semaphore_signal(barrier, inc=1, device_id=d, device_id_type=MESH)

        pl.semaphore_signal(barrier, inc=1, device_id=other, device_id_type=MESH)

    ids = ids_ref[...]
    g = ids // 8
    rel = ((g // 16 - x) & 3) * 16 + ((g // 4 - y) & 3) * 4 + ((g - zh) & 3)
    hot = (lax.broadcasted_iota(jnp.int32, (G, RD), 0) == rel).astype(F32)
    onehot[...] = hot
    before = (
        lax.broadcasted_iota(jnp.int32, (RD, RD), 0) < lax.broadcasted_iota(jnp.int32, (RD, RD), 1)
    ).astype(F32).astype(BF16)
    counts = jnp.dot(hot.astype(BF16), before, preferred_element_type=F32)
    rank = jnp.sum(counts * hot, axis=0, keepdims=True).astype(jnp.int32)
    slot = rel * CAP + rank
    lane = ((rel & 7) * 2 + par) * CAP + rank
    at_lane = (lax.broadcasted_iota(jnp.int32, (B, RD), 0) == lane).astype(F32).astype(BF16)
    lanes[...] = at_lane
    idsend[:, 0, :] = nt((hot * ((ids & 7) + 1).astype(F32)).astype(BF16), at_lane)

    pl.semaphore_wait(barrier, 64)

    def row_copy(i):
        tx, ty, th = (x + i // 16) % 4, (y + i // 4) % 4, (zh + i) % 4
        to = place(tx, ty, 2 * th + (tx + ty) % 2, c)
        k, s = i // 8, 2 * i + par
        return (
            pltpu.make_async_remote_copy(
                send.at[pl.ds(3 * i, 3)], recv.at[pl.ds(3 * s, 3)], s_rows, r_rows.at[k],
                device_id=to, device_id_type=MESH),
            pltpu.make_async_remote_copy(
                idsend.at[i], idrecv.at[s], s_ids, r_ids.at[k], device_id=to, device_id_type=MESH),
        )

    @pl.loop(0, NCH)
    def _(q):
        pick = lax.broadcasted_iota(jnp.int32, (8 * CAP, RD), 0) + q * (8 * CAP) == slot
        rows = jnp.dot(pick.astype(F32).astype(BF16), emb_ref[...], preferred_element_type=F32)
        send[pl.ds(q * 24, 24)] = rows.astype(BF16).reshape(24, 8, D)

        @pl.loop(0, 8)
        def _(n):
            i = q * 8 + n
            mine = jnp.logical_and(owner, i == 0)

            @pl.when(jnp.logical_not(mine))
            def _():
                for copy in row_copy(i):
                    copy.start()

            @pl.when(mine)
            def _():
                pltpu.make_async_copy(send.at[pl.ds(0, 3)], recv.at[pl.ds(3 * par, 3)], r_rows.at[0]).start()
                pltpu.make_async_copy(idsend.at[0], idrecv.at[par], r_ids.at[0]).start()

    @pl.when(owner)
    def _():
        colmax[...] = jnp.full(colmax.shape, -1.0, F32)

        @pl.loop(0, NCH)
        def _(k):
            chunk = recv.at[pl.ds(k * 48, 48)]
            local_wait(chunk, r_rows.at[k])
            joint[k, pl.ds(0, B), :] = chunk[...].reshape(B, D)
            pltpu.make_async_remote_copy(
                joint.at[k, pl.ds(0, B)], joint.at[k, pl.ds(B, B)], s_joint, r_joint.at[k],
                device_id=other, device_id_type=MESH).start()
            local_wait(idrecv.at[pl.ds(k * SRC, SRC)], r_ids.at[k])
            id_row = jnp.max(idrecv[pl.ds(k * SRC, SRC)], axis=0)
            mine = joint[k, pl.ds(0, B), :]
            gram = nt(mine, mine)
            eye = lax.broadcasted_iota(jnp.int32, (B, B), 0) == lax.broadcasted_iota(jnp.int32, (B, B), 1)
            squares = jnp.where(eye, gram, 0.0)
            scale_row = lax.rsqrt(jnp.sum(squares, axis=0, keepdims=True) / D + 1e-6) / math.sqrt(D)
            scale_col = lax.rsqrt(jnp.sum(squares, axis=1, keepdims=True) / D + 1e-6) / math.sqrt(D)
            id_col = jnp.sum(jnp.where(eye, id_row, 0.0), axis=1, keepdims=True)
            meta[k, 0, :, pl.ds(0, B)] = id_row
            meta[k, 1, :, pl.ds(0, B)] = scale_row
            pltpu.make_async_remote_copy(
                meta.at[k, :, :, pl.ds(0, B)], meta.at[k, :, :, pl.ds(B, B)], s_meta, r_meta.at[k],
                device_id=other, device_id_type=MESH).start()
            scol[...] = jnp.broadcast_to(scale_col, (B, 128))
            icol[...] = jnp.broadcast_to(id_col, (B, 128))
            row, _ = pair_max(gram, scol[...], icol[...], scale_row, id_row, eye)
            rowmax[...] = row

            @pl.loop(0, k)
            def _(j):
                for n in range(3):
                    at = pl.ds(256 * n, 256)
                    v = nt(joint[k, pl.ds(0, B), :], joint[j, at, :])
                    row, col = pair_max(v, scol[...], icol[...], meta[j, 1, :, at], meta[j, 0, :, at])
                    rowmax[...] = jnp.maximum(rowmax[...], row)
                    colmax[j, :, at] = jnp.maximum(colmax[j, :, at], col)

            local_wait(joint.at[k, pl.ds(B, B)], r_joint.at[k])
            local_wait(meta.at[k, :, :, pl.ds(B, B)], r_meta.at[k])
            v = nt(joint[k, pl.ds(0, B), :], joint[k, pl.ds(B, B), :])
            row, _ = pair_max(v, scol[...], icol[...], meta[k, 1, :, pl.ds(B, B)], meta[k, 0, :, pl.ds(B, B)])
            row = jnp.maximum(rowmax[...], row)
            best = jnp.max(row.T, axis=0, keepdims=True)
            colmax[k, :, pl.ds(0, B)] = jnp.maximum(colmax[k, :, pl.ds(0, B)], best)

        part = pltpu.make_async_remote_copy(
            colmax.at[:, :, pl.ds(B, B)], theirs, s_part, r_part, device_id=other, device_id_type=MESH)
        part.start()
        part.wait()
        answer[...] = jnp.maximum(colmax[:, :, pl.ds(0, B)], theirs[...])

        @pl.loop(0, 2 * G)
        def _(s):
            i, p = s // 2, s % 2
            mine = jnp.logical_and(i == 0, p == par)
            to = place((x - i // 16 + 4) % 4, (y - (i // 4) % 4 + 4) % 4, 2 * ((zh - i % 4 + 4) % 4) + p, c)

            @pl.when(jnp.logical_not(mine))
            def _():
                pltpu.make_async_remote_copy(
                    answer.at[i // 8], back.at[i], s_ans, r_ans, device_id=to, device_id_type=MESH).start()

            @pl.when(mine)
            def _():
                pltpu.make_async_copy(answer.at[0], back.at[0], r_ans).start()

        local_wait(joint.at[:, pl.ds(0, B)], s_joint)
        local_wait(meta.at[:, :, :, pl.ds(0, B)], s_meta)
        local_wait(idrecv.at[pl.ds(0, 127)], s_ans)
        local_wait(send.at[pl.ds(0, 189)], s_rows)
        local_wait(idsend.at[pl.ds(0, 63)], s_ids)

    @pl.when(jnp.logical_not(owner))
    def _():
        local_wait(send, s_rows)
        local_wait(idsend, s_ids)

    local_wait(back, r_ans)
    rest = back[:, 0, :]
    total = None
    for _ in range(3):
        term = rest.astype(BF16)
        rest = rest - term.astype(F32)
        found = jnp.dot(term, lanes[...], preferred_element_type=F32)
        total = found if total is None else total + found
    out_ref[...] = jnp.sum(total * onehot[...], axis=0, keepdims=True)


def on_device(embeddings, cluster_ids):
    dma = pltpu.SemaphoreType.DMA
    best = pl.pallas_call(
        kernel,
        out_shape=jax.ShapeDtypeStruct((1, RD), F32),
        in_specs=[pl.BlockSpec(memory_space=pltpu.VMEM)] * 2,
        out_specs=pl.BlockSpec(memory_space=pltpu.VMEM),
        scratch_shapes=[
            pltpu.VMEM((G * 3, 8, D), BF16),
            pltpu.VMEM((G, 1, B), F32),
            pltpu.VMEM((G, RD), F32),
            pltpu.VMEM((B, RD), BF16),
            pltpu.VMEM((2 * G * 3, 8, D), BF16),
            pltpu.VMEM((2 * G, 1, B), F32),
            pltpu.VMEM((NCH, 2 * B, D), BF16),
            pltpu.VMEM((NCH, 2, 1, 2 * B), F32),
            pltpu.VMEM((NCH, 1, 2 * B), F32),
            pltpu.VMEM((NCH, 1, B), F32),
            pltpu.VMEM((NCH, 1, B), F32),
            pltpu.VMEM((G, 1, B), F32),
            pltpu.VMEM((B, 128), F32),
            pltpu.VMEM((B, 128), F32),
            pltpu.VMEM((B, 128), F32),
            dma, dma, dma((NCH,)), dma((NCH,)), dma, dma, dma((NCH,)), dma((NCH,)), dma, dma, dma, dma,
        ],
        compiler_params=pltpu.CompilerParams(
            collective_id=0, has_side_effects=True, vmem_limit_bytes=48 << 20
        ),
        name="semdedup",
    )(cluster_ids.reshape(1, RD), embeddings)
    return best.reshape(RD)


def solution(mesh):
    placed = (P(("dp", "grp"), None), P(("dp", "grp")))
    return jax.shard_map(
        on_device, mesh=mesh, in_specs=placed, out_specs=P(("dp", "grp")), check_vma=False
    )
```

time: 284 us -> 106 us (0.37)
  waiting for transfers between devices: 133 us -> 0 us
  Pallas kernels: 0 us -> 103 us
  blocking collectives: 86.2 us -> 0 us
  matrix products: 23.8 us -> 0 us
  local copies, waits for them, and re-layouts: 19.7 us -> 1.96 us
  starting transfers between devices: 12.2 us -> 0 us
  other arithmetic: 8.34 us -> 0.61 us
    ppermute x6 -> x0, waiting for transfers between devices: 123 us -> none  [from_behind(): return lax.ppermute(x, axis, [(i, (i + by) % peers) for i in range(peers)])]
    pallas_call x0 -> x1, Pallas kernels: none -> 103 us  [on_device(): pl.pallas_call(kernel, out_shape=jax.ShapeDtypeStruct((1, RD), F32), in_s...]
    all_to_all x2 -> x0, blocking collectives: 86.2 us -> none  [the longest x1 70.1 us: on_device(): lax.all_to_all(buffer_rows, 'dp', split_axis=0, concat_axis=0, tiled=True)]
    dot_general x5 -> x0, matrix products: 23.8 us -> none  [the longest x4 23.4 us: masked_cosines(): lax.dot_general(own_rows, other_rows, (((1,), (1,)), ((), ())), preferred...]
    scatter x2 -> x0, local copies, waits for them, and re-layouts: 11.5 us -> none  [the longest x1 7.93 us: on_device(): jnp.zeros((dp_size * capacity, embeddings.shape[1]), jnp.bfloat16).at[slots]]
    all_to_all x1 -> x0, starting transfers between devices: 9.61 us -> none  [on_device(): lax.all_to_all(best_sim, 'dp', split_axis=0, concat_axis=0, tiled=True)]
    all_to_all x1 -> x0, waiting for transfers between devices: 9.27 us -> none  [on_device(): lax.all_to_all(best_sim, 'dp', split_axis=0, concat_axis=0, tiled=True)]
    gather x1 -> x0, local copies, waits for them, and re-layouts: 6.15 us -> none  [on_device(): return answers[slots]]
  transfers between devices with their start and end apart: 7 -> 0, of which waited for: 5 -> 0; matrix products, arithmetic and copies ran while one was open for 10% -> 0% of each run, Pallas kernels for 0% -> 0%
where the time goes in v1:
time: 106 us
  Pallas kernels  103 us (97%)
  local copies, waits for them, and re-layouts  1.96 us (2%)
    pallas_call x1, Pallas kernels, on_device(): pl.pallas_call(kernel, out_shape=jax.ShapeDtypeStruct((1, RD), F32), in_s...  103 us

profile of v1, /device:TPU:1, one launch (start us, length us, event | category | flops | bytes accessed | tf_op | source)
XLA Modules:
  0.0 105.9 jit_solution(3321881127282883155)
XLA Ops:
  0.0 0.7 reshape.6.ids_ref
  0.7 0.0 copy-start
  0.7 1.3 %copy-done = bf16[768,768]{1,0:T(8,128)(2,1)S(1)} copy-done((bf16[768,768]{1,0:T(8,128)(2,1)S(1)}, bf16[768,768]{1,0:T(8,128)(2,1)}, u32[]{:S(2)}) %copy-start) | copy-done | bytes 1179672
  2.0 103.4 %semdedup.1 = f32[1,768]{1,0:T(1,128)S(1)} custom-call(s32[1,768]{1,0:T(1,128)S(1)} %reshape.6.ids_ref, bf16[768,768]{1,0:T(8,128)(2,1)S(1)} %copy-done), custom_call_target="tpu_custom_call" | custom-call | tf_op jit(solution)/shard_map/semdedup/pallas_call | solution.py:212
  105.3 0.6 reduce
Async XLA Ops:
  0.7 1.3 %copy-start = (bf16[768,768]{1,0:T(8,128)(2,1)S(1)}, bf16[768,768]{1,0:T(8,128)(2,1)}, u32[]{:S(2)}) copy-start(bf16[768,768]{1,0:T(8,128)(2,1)} %emb_ref.1) | copy-start | bytes 3538948

commit v2 on v1

v2 whole, which is shorter than its diff:
```python
import math

import jax
import jax.numpy as jnp
from jax import lax
from jax.experimental import pallas as pl
from jax.experimental.pallas import tpu as pltpu
from jax.sharding import PartitionSpec as P

D = 768
RD = 768
G = 64
CAP = 24
NCH = 8
AHEAD = 6
SRC = 16
B = SRC * CAP
MESH = pl.DeviceIdType.MESH
F32, BF16 = jnp.float32, jnp.bfloat16


COLUMNS = (
    (0, 0), (2, 2), (1, 3), (3, 1), (1, 1), (3, 3), (0, 1), (0, 3),
    (1, 0), (3, 0), (0, 2), (2, 0), (1, 2), (3, 2), (2, 1), (2, 3),
)


def offset(t):
    def pick(which):
        out = jnp.int32(0)
        for n, xy in enumerate(COLUMNS):
            if xy[which]:
                out = jnp.where(t == n, xy[which], out)
        return out

    return pick(0), pick(1)


def lookup(dx, dy):
    out = jnp.zeros_like(dx)
    for n, xy in enumerate(COLUMNS):
        out = jnp.where((dx == xy[0]) & (dy == xy[1]), n, out)
    return out


def place(x, y, z, c):
    return ((y * 8 + z) * 2 + c, x)


def local_wait(ref, sem):
    pltpu.make_async_copy(ref, ref, sem).wait()


def pair_max(v, scale_col, id_col, scale_row, id_row, itself=None):
    row, cols = None, []
    for t in range(v.shape[1] // 128):
        at = slice(128 * t, 128 * (t + 1))
        same = id_col == id_row[:, at]
        if itself is not None:
            same = same & ~itself[:, at]
        m = jnp.where(same, v[:, at] * scale_col * scale_row[:, at], -1.0)
        row = m if row is None else jnp.maximum(row, m)
        cols.append(jnp.max(m, axis=0, keepdims=True))
    return row, jnp.concatenate(cols, axis=1)


def nt(a, b):
    return lax.dot_general(a, b, (((1,), (1,)), ((), ())), preferred_element_type=F32)


def kernel(
    ids_hbm, emb_hbm, out_ref,
    ids_ref, emb, send, idsend, idline, idlayer, idrecv, hot, lanes, recv, joint, meta, colmax, half, whole, back,
    scol, icol, rowmax,
    ready, s_in, s_rows, s_ids, s_idl, s_joint, s_meta, s_half, s_whole,
    r_rows, r_ids, r_idl, r_joint, r_meta, r_half, r_whole,
):
    dp, x = lax.axis_index("dp"), lax.axis_index("grp")
    y, z, c = dp // 16, (dp // 2) % 8, dp % 2
    zh, par = z // 2, z % 2
    owner = (x + y + z) % 2 == 0
    me_in_layer = x * 2 + y // 2
    other = place(x, y, z, 1 - c)

    def remote(src, dst, ssem, rsem, to):
        return pltpu.make_async_remote_copy(src, dst, ssem, rsem, device_id=to, device_id_type=MESH)

    def signal(sem, to):
        pl.semaphore_signal(sem, inc=1, device_id=to, device_id_type=MESH)

    get_ids = pltpu.make_async_copy(ids_hbm, ids_ref, s_in.at[0])
    get_ids.start()
    get_emb = pltpu.make_async_copy(emb_hbm, emb, s_in.at[1])
    get_emb.start()

    barrier = pltpu.get_barrier_semaphore()

    @pl.loop(1, 8)
    def _(t):
        signal(barrier, place(x, y, (z + t) % 8, c))

    @pl.when(owner)
    def _():
        signal(barrier, other)

        @pl.loop(1, 16)
        def _(t):
            signal(barrier, place((x + t // 4) % 4, (y + t) % 4, z, c))

    get_ids.wait()
    ids = ids_ref[...].reshape(1, RD)
    g = ids // 8
    gx, gy, gh = g // 16, (g // 4) & 3, g & 3
    col = lookup((gx - x) & 3, (gy - y) & 3)
    dh = (gh - zh) & 3
    line = ((2 * gh + ((gx + gy) & 1) - z) & 7) * 8 + gx * 2 + gy // 2
    mask = (lax.broadcasted_iota(jnp.int32, (G, RD), 0) == line).astype(F32)
    hot[...] = mask
    before = (
        lax.broadcasted_iota(jnp.int32, (RD, RD), 0) < lax.broadcasted_iota(jnp.int32, (RD, RD), 1)
    ).astype(F32).astype(BF16)
    counts = jnp.dot(mask.astype(BF16), before, preferred_element_type=F32)
    rank = jnp.sum(counts * mask, axis=0, keepdims=True).astype(jnp.int32)
    slot = (col * 4 + dh) * CAP + rank
    lane = ((col & 1) * 8 + dh * 2 + par) * CAP + rank
    at_lane = (lax.broadcasted_iota(jnp.int32, (B, RD), 0) == lane).astype(F32).astype(BF16)
    lanes[...] = at_lane
    idsend[:, 0, :] = nt((mask * ((ids & 7) + 1).astype(F32)).astype(BF16), at_lane)

    get_emb.wait()

    @pl.loop(0, NCH)
    def _(q):
        pick = lax.broadcasted_iota(jnp.int32, (8 * CAP, RD), 0) + q * (8 * CAP) == slot
        rows = jnp.dot(pick.astype(F32).astype(BF16), emb[...], preferred_element_type=F32)
        send[pl.ds(q * 24, 24)] = rows.astype(BF16).reshape(24, 8, D)

    pl.semaphore_wait(barrier, 15)

    @pl.loop(1, 8)
    def _(t):
        signal(ready, place(x, y, (z + t) % 8, c))

    @pl.loop(1, 8)
    def _(t):
        remote(idsend.at[pl.ds(8 * t, 8)], idline.at[t - 1], s_ids, r_ids, place(x, y, (z + t) % 8, c)).start()

    def issue(q):
        @pl.loop(0, 8)
        def _(n):
            i = q * 8 + n
            dx, dy = offset(i // 4)
            tx, ty = (x + dx) % 4, (y + dy) % 4
            k, at = i // 8, 2 * i + par
            mine = jnp.logical_and(owner, i == 0)

            @pl.when(jnp.logical_not(mine))
            def _():
                to = place(tx, ty, 2 * ((zh + i) % 4) + (tx + ty) % 2, c)
                remote(send.at[pl.ds(3 * i, 3)], recv.at[pl.ds(3 * at, 3)], s_rows.at[k], r_rows.at[k], to).start()

            @pl.when(mine)
            def _():
                pltpu.make_async_copy(send.at[pl.ds(0, 3)], recv.at[pl.ds(3 * par, 3)], r_rows.at[0]).start()

    def sent(q):
        @pl.when(jnp.logical_and(owner, q == 0))
        def _():
            local_wait(send.at[pl.ds(0, 21)], s_rows.at[0])

        @pl.when(jnp.logical_not(jnp.logical_and(owner, q == 0)))
        def _():
            local_wait(send.at[pl.ds(0, 24)], s_rows.at[q])

    pl.semaphore_wait(ready, 7)

    @pl.loop(0, AHEAD)
    def _(q):
        issue(q)

    local_wait(idline, r_ids)
    idlayer[...] = jnp.maximum(idsend[pl.ds(0, 8)], jnp.max(idline[...], axis=0))

    @pl.loop(0, 16)
    def _(t):
        dx, dy = offset(t)
        tx, ty = (x + dx) % 4, (y + dy) % 4

        @pl.when(jnp.logical_and((tx + ty + z) % 2 == 0, t > 0))
        def _():
            remote(idlayer.at[tx * 2 + ty // 2], idrecv.at[t], s_idl, r_idl, place(tx, ty, z, c)).start()

    @pl.when(jnp.logical_not(owner))
    def _():
        @pl.loop(AHEAD, NCH)
        def _(q):
            sent(q - AHEAD)
            issue(q)

    @pl.when(owner)
    def _():
        colmax[...] = jnp.full(colmax.shape, -1.0, F32)
        idrecv[0] = idlayer[me_in_layer]
        local_wait(idrecv.at[pl.ds(1, 15)], r_idl)

        def finish(k):
            local_wait(joint.at[k, pl.ds(B, B)], r_joint.at[k])
            local_wait(meta.at[k, :, :, pl.ds(B, B)], r_meta.at[k])
            v = nt(joint[k, pl.ds(0, B), :], joint[k, pl.ds(B, B), :])
            at = pl.ds(B, B)
            row, _ = pair_max(v, scol[k % 2], icol[k % 2], meta[k, 1, :, at], meta[k, 0, :, at])
            row = jnp.maximum(rowmax[k % 2], row)
            best = jnp.max(row.T, axis=0, keepdims=True)
            colmax[k, :, pl.ds(0, B)] = jnp.maximum(colmax[k, :, pl.ds(0, B)], best)

        @pl.loop(0, NCH)
        def _(k):
            chunk = recv.at[pl.ds(k * 48, 48)]
            @pl.when(k + AHEAD < NCH)
            def _():
                sent(k)
                issue(k + AHEAD)

            local_wait(chunk, r_rows.at[k])
            joint[k, pl.ds(0, B), :] = chunk[...].reshape(B, D)
            remote(joint.at[k, pl.ds(0, B)], joint.at[k, pl.ds(B, B)], s_joint, r_joint.at[k], other).start()
            id_row = jnp.maximum(idrecv[2 * k], idrecv[2 * k + 1])
            mine = joint[k, pl.ds(0, B), :]
            gram = nt(mine, mine)
            eye = lax.broadcasted_iota(jnp.int32, (B, B), 0) == lax.broadcasted_iota(jnp.int32, (B, B), 1)
            squares = jnp.where(eye, gram, 0.0)
            scale_row = lax.rsqrt(jnp.sum(squares, axis=0, keepdims=True) / D + 1e-6) / math.sqrt(D)
            scale_col = lax.rsqrt(jnp.sum(squares, axis=1, keepdims=True) / D + 1e-6) / math.sqrt(D)
            id_col = jnp.sum(jnp.where(eye, id_row, 0.0), axis=1, keepdims=True)
            meta[k, 0, :, pl.ds(0, B)] = id_row
            meta[k, 1, :, pl.ds(0, B)] = scale_row
            remote(
                meta.at[k, :, :, pl.ds(0, B)], meta.at[k, :, :, pl.ds(B, B)], s_meta, r_meta.at[k], other
            ).start()
            scol[k % 2] = jnp.broadcast_to(scale_col, (B, 128))
            icol[k % 2] = jnp.broadcast_to(id_col, (B, 128))
            row, _ = pair_max(gram, scol[k % 2], icol[k % 2], scale_row, id_row, eye)
            rowmax[k % 2] = row

            @pl.when(k > 0)
            def _():
                finish(k - 1)

            def cross(*chunks):
                best = rowmax[k % 2]
                for j in chunks:
                    for n in range(3):
                        at = pl.ds(256 * n, 256)
                        v = nt(joint[k, pl.ds(0, B), :], joint[j, at, :])
                        row, col = pair_max(v, scol[k % 2], icol[k % 2], meta[j, 1, :, at], meta[j, 0, :, at])
                        best = jnp.maximum(best, row)
                        colmax[j, :, at] = jnp.maximum(colmax[j, :, at], col)
                rowmax[k % 2] = best

            @pl.loop(0, k // 2)
            def _(j):
                cross(2 * j, 2 * j + 1)

            @pl.when(k % 2 == 1)
            def _():
                cross(k - 1)

        finish(NCH - 1)

        half[2 * me_in_layer + c] = colmax[0, :, pl.ds(0, B)]

        @pl.loop(0, 16)
        def _(t):
            dx, dy = offset(t)
            hx, hy = (x - dx + 4) % 4, (y - dy + 4) % 4
            into = half.at[2 * me_in_layer + c]
            remote(colmax.at[t // 2, :, pl.ds(B, B)], into, s_half, r_half, place(hx, hy, z, 1 - c)).start()

            @pl.when(t > 0)
            def _():
                remote(colmax.at[t // 2, :, pl.ds(0, B)], into, s_half, r_half, place(hx, hy, z, c)).start()

        local_wait(half.at[pl.ds(0, 15)], r_half)

    @pl.when(jnp.logical_not(owner))
    def _():
        local_wait(half, r_half)

    whole[...] = jnp.max(half[...].reshape(8, 2, 1, B), axis=1)

    @pl.loop(1, 8)
    def _(t):
        remote(whole, back.at[pl.ds(64 - 8 * t, 8)], s_whole, r_whole, place(x, y, (z + t) % 8, c)).start()

    back[pl.ds(0, 8)] = whole[...]

    local_wait(idline, s_ids)

    @pl.loop(NCH - AHEAD, NCH)
    def _(q):
        sent(q)

    @pl.when(owner)
    def _():
        local_wait(idlayer.at[pl.ds(0, 7)], s_idl)
        local_wait(joint.at[:, pl.ds(0, B)], s_joint)
        local_wait(meta.at[:, :, :, pl.ds(0, B)], s_meta)
        local_wait(idsend.at[pl.ds(0, 31)], s_half)

    @pl.when(jnp.logical_not(owner))
    def _():
        local_wait(idlayer, s_idl)

    local_wait(back.at[pl.ds(8, 56)], r_whole)
    local_wait(back.at[pl.ds(8, 56)], s_whole)
    rest = back[:, 0, :]
    total = None
    for _ in range(3):
        term = rest.astype(BF16)
        rest = rest - term.astype(F32)
        found = jnp.dot(term, lanes[...], preferred_element_type=F32)
        total = found if total is None else total + found
    out_ref[...] = jnp.sum(total * hot[...], axis=0, keepdims=True).reshape(RD)


def on_device(embeddings, cluster_ids):
    dma = pltpu.SemaphoreType.DMA
    return pl.pallas_call(
        kernel,
        out_shape=jax.ShapeDtypeStruct((RD,), F32),
        in_specs=[pl.BlockSpec(memory_space=pltpu.HBM)] * 2,
        out_specs=pl.BlockSpec(memory_space=pltpu.VMEM),
        scratch_shapes=[
            pltpu.VMEM((RD,), jnp.int32),
            pltpu.VMEM((RD, D), BF16),
            pltpu.VMEM((G * 3, 8, D), BF16),
            pltpu.VMEM((G, 1, B), F32),
            pltpu.VMEM((7, 8, 1, B), F32),
            pltpu.VMEM((8, 1, B), F32),
            pltpu.VMEM((16, 1, B), F32),
            pltpu.VMEM((G, RD), F32),
            pltpu.VMEM((B, RD), BF16),
            pltpu.VMEM((2 * G * 3, 8, D), BF16),
            pltpu.VMEM((NCH, 2 * B, D), BF16),
            pltpu.VMEM((NCH, 2, 1, 2 * B), F32),
            pltpu.VMEM((NCH, 1, 2 * B), F32),
            pltpu.VMEM((16, 1, B), F32),
            pltpu.VMEM((8, 1, B), F32),
            pltpu.VMEM((G, 1, B), F32),
            pltpu.VMEM((2, B, 128), F32),
            pltpu.VMEM((2, B, 128), F32),
            pltpu.VMEM((2, B, 128), F32),
            pltpu.SemaphoreType.REGULAR, dma((2,)), dma((NCH,)), dma, dma, dma, dma, dma, dma,
            dma((NCH,)), dma, dma, dma((NCH,)), dma((NCH,)), dma, dma,
        ],
        compiler_params=pltpu.CompilerParams(
            collective_id=0, has_side_effects=True, vmem_limit_bytes=48 << 20
        ),
        name="semdedup",
    )(cluster_ids, embeddings)


def solution(mesh):
    placed = (P(("dp", "grp"), None), P(("dp", "grp")))
    return jax.shard_map(
        on_device, mesh=mesh, in_specs=placed, out_specs=P(("dp", "grp")), check_vma=False
    )
```

time: 106 us -> 96 us (0.906)
  Pallas kernels: 103 us -> 93.3 us
    pallas_call x1, Pallas kernels: 103 us -> 93.3 us  [on_device(): pl.pallas_call(kernel, out_shape=jax.ShapeDtypeStruct((RD,), F32), in_spe...]
    unnamed x2 -> x5, local copies, waits for them, and re-layouts: 1.27 us -> 2.55 us
where the time goes in v2:
time: 96 us; the launch traced here: 95.8 us
  Pallas kernels  93.3 us (97%)
  local copies, waits for them, and re-layouts  2.55 us (3%)
    pallas_call x1, Pallas kernels, on_device(): pl.pallas_call(kernel, out_shape=jax.ShapeDtypeStruct((RD,), F32), in_spe...  93.3 us
    unnamed x5, local copies, waits for them, and re-layouts  2.55 us

profile of v2, /device:TPU:1, one launch (start us, length us, event | category | flops | bytes accessed | tf_op | source)
XLA Modules:
  0.0 95.8 jit_solution(12312124970055952130)
XLA Ops:
  0.0 0.0 copy-start
  0.0 1.3 %copy-done = bf16[768,768]{1,0:T(8,128)(2,1)S(1)} copy-done((bf16[768,768]{1,0:T(8,128)(2,1)S(1)}, bf16[768,768]{1,0:T(8,128)(2,1)}, u32[]{:S(2)}) %copy-start) | copy-done | bytes 1179672
  1.3 0.0 copy-start.1
  1.3 0.7 copy-done.1
  2.0 93.3 %semdedup.1 = f32[768]{0:T(1024)S(1)} custom-call(s32[768]{0:T(1024)S(1)} %copy-done.1, bf16[768,768]{1,0:T(8,128)(2,1)S(1)} %copy-done), custom_call_target="tpu_custom_call" | custom-call | tf_op jit(solution)/shard_map/semdedup/pallas_call | solution.py:328
  95.2 0.6 copy.4
Async XLA Ops:
  0.0 1.3 %copy-start = (bf16[768,768]{1,0:T(8,128)(2,1)S(1)}, bf16[768,768]{1,0:T(8,128)(2,1)}, u32[]{:S(2)}) copy-start(bf16[768,768]{1,0:T(8,128)(2,1)} %emb_hbm.1) | copy-start | bytes 3538948
  1.3 0.7 copy-start.1

commit v3 on v2

--- a/solution.py
+++ b/solution.py
@@ -12,7 +12,6 @@
 G = 64
 CAP = 24
 NCH = 8
-AHEAD = 6
 SRC = 16
 B = SRC * CAP
 MESH = pl.DeviceIdType.MESH
@@ -145,38 +144,43 @@
     def _(t):
         remote(idsend.at[pl.ds(8 * t, 8)], idline.at[t - 1], s_ids, r_ids, place(x, y, (z + t) % 8, c)).start()
 
-    def issue(q):
-        @pl.loop(0, 8)
-        def _(n):
-            i = q * 8 + n
-            dx, dy = offset(i // 4)
-            tx, ty = (x + dx) % 4, (y + dy) % 4
-            k, at = i // 8, 2 * i + par
-            mine = jnp.logical_and(owner, i == 0)
-
-            @pl.when(jnp.logical_not(mine))
-            def _():
-                to = place(tx, ty, 2 * ((zh + i) % 4) + (tx + ty) % 2, c)
-                remote(send.at[pl.ds(3 * i, 3)], recv.at[pl.ds(3 * at, 3)], s_rows.at[k], r_rows.at[k], to).start()
-
-            @pl.when(mine)
-            def _():
-                pltpu.make_async_copy(send.at[pl.ds(0, 3)], recv.at[pl.ds(3 * par, 3)], r_rows.at[0]).start()
-
-    def sent(q):
-        @pl.when(jnp.logical_and(owner, q == 0))
+    def row_copy(i):
+        dx, dy = offset(i // 4)
+        tx, ty, tz = (x + dx) % 4, (y + dy) % 4, 2 * ((zh + i) % 4)
+        tz = tz + (tx + ty) % 2
+        k, at = i // 8, 2 * i + par
+        copy = remote(
+            send.at[pl.ds(3 * i, 3)], recv.at[pl.ds(3 * at, 3)], s_rows, r_rows.at[k], place(tx, ty, tz, c)
+        )
+        return copy, jnp.logical_or(i < 4, tz == z)
+
+    @pl.when(owner)
+    def _():
+        pltpu.make_async_copy(send.at[pl.ds(0, 3)], recv.at[pl.ds(3 * par, 3)], r_rows.at[0]).start()
+
+    @pl.loop(0, 4)
+    def _(i):
+        @pl.when(jnp.logical_not(jnp.logical_and(owner, i == 0)))
         def _():
-            local_wait(send.at[pl.ds(0, 21)], s_rows.at[0])
-
-        @pl.when(jnp.logical_not(jnp.logical_and(owner, q == 0)))
+            row_copy(i)[0].start()
+
+    @pl.loop(1, 16)
+    def _(t):
+        copy, near = row_copy(4 * t)
+
+        @pl.when(near)
         def _():
-            local_wait(send.at[pl.ds(0, 24)], s_rows.at[q])
+            copy.start()
 
     pl.semaphore_wait(ready, 7)
 
-    @pl.loop(0, AHEAD)
-    def _(q):
-        issue(q)
+    @pl.loop(0, G)
+    def _(n):
+        copy, near = row_copy(n)
+
+        @pl.when(jnp.logical_not(near))
+        def _():
+            copy.start()
 
     local_wait(idline, r_ids)
     idlayer[...] = jnp.maximum(idsend[pl.ds(0, 8)], jnp.max(idline[...], axis=0))
@@ -189,13 +193,6 @@
         @pl.when(jnp.logical_and((tx + ty + z) % 2 == 0, t > 0))
         def _():
             remote(idlayer.at[tx * 2 + ty // 2], idrecv.at[t], s_idl, r_idl, place(tx, ty, z, c)).start()
-
-    @pl.when(jnp.logical_not(owner))
-    def _():
-        @pl.loop(AHEAD, NCH)
-        def _(q):
-            sent(q - AHEAD)
-            issue(q)
 
     @pl.when(owner)
     def _():
@@ -216,11 +213,6 @@
         @pl.loop(0, NCH)
         def _(k):
             chunk = recv.at[pl.ds(k * 48, 48)]
-            @pl.when(k + AHEAD < NCH)
-            def _():
-                sent(k)
-                issue(k + AHEAD)
-
             local_wait(chunk, r_rows.at[k])
             joint[k, pl.ds(0, B), :] = chunk[...].reshape(B, D)
             remote(joint.at[k, pl.ds(0, B)], joint.at[k, pl.ds(B, B)], s_joint, r_joint.at[k], other).start()
@@ -257,9 +249,13 @@
                         colmax[j, :, at] = jnp.maximum(colmax[j, :, at], col)
                 rowmax[k % 2] = best
 
-            @pl.loop(0, k // 2)
+            @pl.loop(0, k // 4)
             def _(j):
-                cross(2 * j, 2 * j + 1)
+                cross(4 * j, 4 * j + 1, 4 * j + 2, 4 * j + 3)
+
+            @pl.when(k % 4 >= 2)
+            def _():
+                cross(k // 4 * 4, k // 4 * 4 + 1)
 
             @pl.when(k % 2 == 1)
             def _():
@@ -269,15 +265,11 @@
 
         half[2 * me_in_layer + c] = colmax[0, :, pl.ds(0, B)]
 
-        @pl.loop(0, 16)
-        def _(t):
-            dx, dy = offset(t)
-            hx, hy = (x - dx + 4) % 4, (y - dy + 4) % 4
-            into = half.at[2 * me_in_layer + c]
+        into = half.at[2 * me_in_layer + c]
+        for t, (dx, dy) in enumerate(COLUMNS):
+            hx, hy = (x + 4 - dx) % 4, (y + 4 - dy) % 4
             remote(colmax.at[t // 2, :, pl.ds(B, B)], into, s_half, r_half, place(hx, hy, z, 1 - c)).start()
-
-            @pl.when(t > 0)
-            def _():
+            if t > 0:
                 remote(colmax.at[t // 2, :, pl.ds(0, B)], into, s_half, r_half, place(hx, hy, z, c)).start()
 
         local_wait(half.at[pl.ds(0, 15)], r_half)
@@ -288,20 +280,16 @@
 
     whole[...] = jnp.max(half[...].reshape(8, 2, 1, B), axis=1)
 
-    @pl.loop(1, 8)
-    def _(t):
+    for t in (4, 3, 5, 2, 6, 1, 7):
         remote(whole, back.at[pl.ds(64 - 8 * t, 8)], s_whole, r_whole, place(x, y, (z + t) % 8, c)).start()
 
     back[pl.ds(0, 8)] = whole[...]
 
     local_wait(idline, s_ids)
 
-    @pl.loop(NCH - AHEAD, NCH)
-    def _(q):
-        sent(q)
-
     @pl.when(owner)
     def _():
+        local_wait(send.at[pl.ds(0, 189)], s_rows)
         local_wait(idlayer.at[pl.ds(0, 7)], s_idl)
         local_wait(joint.at[:, pl.ds(0, B)], s_joint)
         local_wait(meta.at[:, :, :, pl.ds(0, B)], s_meta)
@@ -309,6 +297,7 @@
 
     @pl.when(jnp.logical_not(owner))
     def _():
+        local_wait(send, s_rows)
         local_wait(idlayer, s_idl)
 
     local_wait(back.at[pl.ds(8, 56)], r_whole)
@@ -350,7 +339,7 @@
             pltpu.VMEM((2, B, 128), F32),
             pltpu.VMEM((2, B, 128), F32),
             pltpu.VMEM((2, B, 128), F32),
-            pltpu.SemaphoreType.REGULAR, dma((2,)), dma((NCH,)), dma, dma, dma, dma, dma, dma,
+            pltpu.SemaphoreType.REGULAR, dma((2,)), dma, dma, dma, dma, dma, dma, dma,
             dma((NCH,)), dma, dma, dma((NCH,)), dma((NCH,)), dma, dma,
         ],
         compiler_params=pltpu.CompilerParams(

time: 96 us -> 92.7 us (0.966)
  Pallas kernels: 93.3 us -> 90 us
    pallas_call x1, Pallas kernels: 93.3 us -> 90 us  [on_device(): pl.pallas_call(kernel, out_shape=jax.ShapeDtypeStruct((RD,), F32), in_spe...]
where the time goes in v3:
time: 92.7 us; the launch traced here: 92.6 us
  Pallas kernels  90 us (97%)
  local copies, waits for them, and re-layouts  2.55 us (3%)
    pallas_call x1, Pallas kernels, on_device(): pl.pallas_call(kernel, out_shape=jax.ShapeDtypeStruct((RD,), F32), in_spe...  90 us
    unnamed x5, local copies, waits for them, and re-layouts  2.55 us

profile of v3, /device:TPU:1, one launch (start us, length us, event | category | flops | bytes accessed | tf_op | source)
XLA Modules:
  0.0 92.6 jit_solution(3125789933719462150)
XLA Ops:
  0.0 0.0 copy-start
  0.0 1.3 %copy-done = bf16[768,768]{1,0:T(8,128)(2,1)S(1)} copy-done((bf16[768,768]{1,0:T(8,128)(2,1)S(1)}, bf16[768,768]{1,0:T(8,128)(2,1)}, u32[]{:S(2)}) %copy-start) | copy-done | bytes 1179672
  1.3 0.0 copy-start.1
  1.3 0.7 copy-done.1
  2.0 90.0 %semdedup.1 = f32[768]{0:T(1024)S(1)} custom-call(s32[768]{0:T(1024)S(1)} %copy-done.1, bf16[768,768]{1,0:T(8,128)(2,1)S(1)} %copy-done), custom_call_target="tpu_custom_call" | custom-call | tf_op jit(solution)/shard_map/semdedup/pallas_call | solution.py:317
  92.0 0.6 copy.4
Async XLA Ops:
  0.0 1.3 %copy-start = (bf16[768,768]{1,0:T(8,128)(2,1)S(1)}, bf16[768,768]{1,0:T(8,128)(2,1)}, u32[]{:S(2)}) copy-start(bf16[768,768]{1,0:T(8,128)(2,1)} %emb_hbm.1) | copy-start | bytes 3538948
  1.3 0.7 copy-start.1

commit v4 on v3

--- a/solution.py
+++ b/solution.py
@@ -128,7 +128,7 @@
 
     get_emb.wait()
 
-    @pl.loop(0, NCH)
+    @pl.loop(0, NCH // 2)
     def _(q):
         pick = lax.broadcasted_iota(jnp.int32, (8 * CAP, RD), 0) + q * (8 * CAP) == slot
         rows = jnp.dot(pick.astype(F32).astype(BF16), emb[...], preferred_element_type=F32)
@@ -143,6 +143,12 @@
     @pl.loop(1, 8)
     def _(t):
         remote(idsend.at[pl.ds(8 * t, 8)], idline.at[t - 1], s_ids, r_ids, place(x, y, (z + t) % 8, c)).start()
+
+    @pl.loop(NCH // 2, NCH)
+    def _(q):
+        pick = lax.broadcasted_iota(jnp.int32, (8 * CAP, RD), 0) + q * (8 * CAP) == slot
+        rows = jnp.dot(pick.astype(F32).astype(BF16), emb[...], preferred_element_type=F32)
+        send[pl.ds(q * 24, 24)] = rows.astype(BF16).reshape(24, 8, D)
 
     def row_copy(i):
         dx, dy = offset(i // 4)
@@ -212,6 +218,10 @@
 
         @pl.loop(0, NCH)
         def _(k):
+            @pl.when(k > 0)
+            def _():
+                finish(k - 1)
+
             chunk = recv.at[pl.ds(k * 48, 48)]
             local_wait(chunk, r_rows.at[k])
             joint[k, pl.ds(0, B), :] = chunk[...].reshape(B, D)
@@ -233,10 +243,6 @@
             icol[k % 2] = jnp.broadcast_to(id_col, (B, 128))
             row, _ = pair_max(gram, scol[k % 2], icol[k % 2], scale_row, id_row, eye)
             rowmax[k % 2] = row
-
-            @pl.when(k > 0)
-            def _():
-                finish(k - 1)
 
             def cross(*chunks):
                 best = rowmax[k % 2]

time: 92.7 us -> 91.6 us (0.988)
  Pallas kernels: 90 us -> 88.9 us
    pallas_call x1, Pallas kernels: 90 us -> 88.9 us  [on_device(): pl.pallas_call(kernel, out_shape=jax.ShapeDtypeStruct((RD,), F32), in_spe...]
where the time goes in v4:
time: 91.6 us; the launch traced here: 91.5 us
  Pallas kernels  88.9 us (97%)
  local copies, waits for them, and re-layouts  2.55 us (3%)
    pallas_call x1, Pallas kernels, on_device(): pl.pallas_call(kernel, out_shape=jax.ShapeDtypeStruct((RD,), F32), in_spe...  88.9 us
    unnamed x5, local copies, waits for them, and re-layouts  2.55 us

profile of v4, /device:TPU:1, one launch (start us, length us, event | category | flops | bytes accessed | tf_op | source)
XLA Modules:
  0.0 91.5 jit_solution(12858301054169686214)
XLA Ops:
  0.0 0.0 copy-start
  0.0 1.3 %copy-done = bf16[768,768]{1,0:T(8,128)(2,1)S(1)} copy-done((bf16[768,768]{1,0:T(8,128)(2,1)S(1)}, bf16[768,768]{1,0:T(8,128)(2,1)}, u32[]{:S(2)}) %copy-start) | copy-done | bytes 1179672
  1.3 0.0 copy-start.1
  1.3 0.7 copy-done.1
  2.0 88.9 %semdedup.1 = f32[768]{0:T(1024)S(1)} custom-call(s32[768]{0:T(1024)S(1)} %copy-done.1, bf16[768,768]{1,0:T(8,128)(2,1)S(1)} %copy-done), custom_call_target="tpu_custom_call" | custom-call | tf_op jit(solution)/shard_map/semdedup/pallas_call | solution.py:323
  90.9 0.6 copy.4
Async XLA Ops:
  0.0 1.3 %copy-start = (bf16[768,768]{1,0:T(8,128)(2,1)S(1)}, bf16[768,768]{1,0:T(8,128)(2,1)}, u32[]{:S(2)}) copy-start(bf16[768,768]{1,0:T(8,128)(2,1)} %emb_hbm.1) | copy-start | bytes 3538948
  1.3 0.7 copy-start.1
